TPU v7x, 32 devices: a whole 2x2x4 slice. The times are simulated.
32 devices in a mesh: row: 8 (over z, x), col: 4 (over y, core).
Axes of the slice: x: 2, y: 2, z: 4, core: 2. Of those that a mesh axis runs over, the one named last changes fastest.
Arguments:
- signal: bfloat16 [16384, 2048], P('row', 'col'), may hold values from -40 to 40
- norm_gain: float32 [2048], replicated, may hold values from 0.5 to 2
- qkv_weight: bfloat16 [2048, 6144], P('row', 'col'), may hold values from -4 to 4
- out_weight: bfloat16 [2048, 2048], P('row', 'col'), may hold values from -1 to 1
Outputs:
- layer_out: bfloat16 [16384, 2048], P('row', 'col')
All inputs are finite; a program needn't handle non-finite values.
Results may differ from a plain program's by a relative error of at most 0.006.
Values may be sent and summed in bfloat16 or wider, within the bound.
A program may use at most 64 MiB of HBM per device.

v0:
```python
import math

import jax
import jax.numpy as jnp
from jax import lax
from jax.sharding import PartitionSpec as P

HS = 128
COLS = 1024


EPSILON = 1e-05
NEGATIVE = -1e30


def row_softmax(row_block):
    head_size = row_block.shape[-1] // 3
    queries = row_block[..., :head_size]
    key_part = row_block[..., head_size : 2 * head_size]
    values = row_block[..., 2 * head_size :]
    factor = 1.0 / math.sqrt(head_size)
    scores = (
        jnp.einsum("chd,ehd->hce", queries, key_part, preferred_element_type=jnp.float32) * factor
    )
    length = row_block.shape[0]
    causal = jnp.arange(length)[:, None] >= jnp.arange(length)[None, :]
    scores = jnp.where(causal, scores, NEGATIVE)
    maxima = jnp.max(scores, axis=-1)
    weights = jnp.where(causal, jnp.exp(scores - maxima[..., None]), 0.0)
    totals = jnp.sum(weights, axis=-1)
    summed = jnp.einsum(
        "hce,ehd->chd", weights.astype(jnp.bfloat16), values, preferred_element_type=jnp.float32
    )
    return (summed, maxima.T, totals.T)


def column_softmax(gathered):
    head_size = gathered.shape[-1] // 3
    queries = gathered[..., :head_size]
    key_part = gathered[..., head_size : 2 * head_size]
    values = gathered[..., 2 * head_size :]
    factor = 1.0 / math.sqrt(head_size)
    scores = (
        jnp.einsum("rchd,schd->chrs", queries, key_part, preferred_element_type=jnp.float32)
        * factor
    )
    length = gathered.shape[0]
    earlier = jnp.arange(length)[:, None] > jnp.arange(length)[None, :]
    scores = jnp.where(earlier, scores, NEGATIVE)
    maxima = jnp.max(scores, axis=-1)
    weights = jnp.where(earlier, jnp.exp(scores - maxima[..., None]), 0.0)
    totals = jnp.sum(weights, axis=-1)
    summed = jnp.einsum(
        "chrs,schd->rchd", weights.astype(jnp.bfloat16), values, preferred_element_type=jnp.float32
    )
    maxima_rows = jnp.transpose(maxima, (2, 0, 1))
    totals_rows = jnp.transpose(totals, (2, 0, 1))
    return (
        lax.all_to_all(summed, "row", split_axis=0, concat_axis=1, tiled=True),
        lax.all_to_all(maxima_rows, "row", split_axis=0, concat_axis=1, tiled=True),
        lax.all_to_all(totals_rows, "row", split_axis=0, concat_axis=1, tiled=True),
    )


def per_device(signal, norm_gain, qkv_weight, out_weight):
    samples = signal.shape[0]
    gathered = lax.all_gather(signal, "col", axis=1, tiled=True)
    widened = gathered.astype(jnp.float32)
    average = jnp.mean(widened, axis=1, keepdims=True)
    variance = jnp.mean((widened - average) ** 2, axis=1, keepdims=True)
    normed = ((widened - average) * lax.rsqrt(variance + EPSILON) * norm_gain).astype(jnp.bfloat16)
    qkv_width = qkv_weight.shape[1]
    piece_qkv = lax.all_gather(qkv_weight, "row", axis=0, tiled=True)
    piece_out = lax.all_gather(out_weight, "row", axis=0, tiled=True)
    projected_sum = jnp.dot(normed, piece_qkv, preferred_element_type=jnp.float32)
    qkv = projected_sum.astype(jnp.bfloat16)
    rows_here = samples // COLS
    heads_here = qkv_width // (3 * HS)
    stacked = qkv.reshape(rows_here, COLS, heads_here, 3 * HS)
    row_acc, row_max, row_total = lax.map(row_softmax, stacked)
    col_acc, col_max, col_total = column_softmax(
        lax.all_to_all(stacked, "row", split_axis=1, concat_axis=0, tiled=True)
    )
    highest = jnp.maximum(row_max, col_max)
    row_factor = jnp.exp(row_max - highest)
    col_factor = jnp.exp(col_max - highest)
    denominator = row_factor * row_total + col_factor * col_total
    merged = (row_factor[..., None] * row_acc + col_factor[..., None] * col_acc) / denominator[
        ..., None
    ]
    attended = merged.astype(jnp.bfloat16).reshape(samples, heads_here * HS)
    residual = signal.astype(jnp.float32)
    branch = jnp.dot(
        lax.all_gather(attended, "col", axis=1, tiled=True),
        piece_out,
        preferred_element_type=jnp.float32,
    )
    return (residual + branch).astype(jnp.bfloat16)


def solution(mesh):
    return jax.shard_map(
        per_device,
        mesh=mesh,
        in_specs=(P("row", "col"), P(), P("row", "col"), P("row", "col")),
        out_specs=P("row", "col"),
        check_vma=False,
    )
```

profile of v0, /device:TPU:0, one launch (start us, length us, event | category | flops | bytes accessed | tf_op | source)
XLA Modules:
  0.0 616.8 jit_solution(10122624546850625512)
XLA Ops:
  6.5 0.7 all-gather.5.cloned.1.call-update
  7.3 0.7 all-gather.7.cloned.1.call-update
  8.0 61.9 %all-gather.5.cloned.1.call-done = bf16[2048,2048]{1,0:T(8,128)(2,1)} async-done(((bf16[2048,512]{1,0:T(8,128)(2,1)}), bf16[2048,2048]{1,0:T(8,128)(2,1)}) %all-gather.5.cloned.1.call-update) | async-done | bytes 8388624 | tf_op jit(solution)/shard_map/all_gather | solution.py:67
  69.9 4.7 convert_reduce_fusion
  74.7 1.1 copy-done.1
  75.7 2.3 fusion.17
  78.0 93.2 %all-gather.7.cloned.1.call-done = bf16[2048,1536]{1,0:T(8,128)(2,1)} async-done(((bf16[256,1536]{1,0:T(8,128)(2,1)}), bf16[2048,1536]{1,0:T(8,128)(2,1)}) %all-gather.7.cloned.1.call-update) | async-done | bytes 6291472 | tf_op jit(solution)/shard_map/all_gather | solution.py:73
  171.2 19.1 %fusion.25 = bf16[2048,1536]{1,0:T(8,128)(2,1)} fusion(bf16[2048,1536]{1,0:T(8,128)(2,1)} %all-gather.7.cloned.1.call-done, bf16[2048,2048]{1,0:T(8,128)(2,1)} %all-gather.5.cloned.1.call-done, f32[2048]{0:T(1024)S(1)} %copy-done.3, f32[2048]{0:T(1024)S(1)} %add_rsqrt_fusion, f32[2048]{0:T(1024)S(1)} %broadcast_multiply_fusion), kind=kOutput, calls=%fused_computation.31 | convolution fusion | flops 12909019136 | bytes 20996096 | tf_op jit(solution)/shard_map/dot_general | solution.py:75
  190.3 11.3 %reshape.24 = bf16[2,1024,4,384]{3,2,1,0:T(4,128)(2,1)} reshape(bf16[2048,1536]{1,0:T(8,128)(2,1)} %fusion.25) | data formatting | bytes 12582912 | tf_op jit(solution)/shard_map/reshape | solution.py:79
  201.6 7.5 %copy.48 = bf16[2,1024,4,384]{3,2,0,1:T(4,128)(2,1)} copy(bf16[2,1024,4,384]{3,2,1,0:T(4,128)(2,1)} %reshape.24) | data formatting | bytes 12582912 | tf_op jit(solution)/shard_map/reshape | solution.py:79
  209.2 4.9 all-to-all-start
  214.1 137.7 %all-to-all-done = bf16[2,1024,4,384]{3,2,0,1:T(4,128)(2,1)} async-done(((bf16[2,1024,4,384]{3,2,0,1:T(4,128)(2,1)}), bf16[2,1024,4,384]{3,2,0,1:T(4,128)(2,1)}, u32[]{:S(2)}, u32[]{:S(2)}) %all-to-all-start) | async-done | bytes 6291488 | tf_op jit(solution)/shard_map/all_to_all | solution.py:82
  351.8 10.3 %copy.78 = bf16[2,8,128,4,384]{4,0,1,3,2:T(2,128)(2,1)} copy(bf16[2,8,128,4,384]{4,3,0,2,1:T(4,128)(2,1)} %bitcast.7) | data formatting | bytes 12582912 | tf_op jit(solution)/shard_map/all_to_all | solution.py:82
  362.1 13.8 %all_to_all.55 = bf16[16,128,4,384]{3,0,2,1:T(8,128)(2,1)} reshape(bf16[8,2,128,4,384]{4,1,0,3,2:T(2,128)(2,1)} %bitcast.76) | data formatting | bytes 12582912 | tf_op jit(solution)/shard_map/all_to_all | solution.py:82
  375.9 5.4 fusion.29
  381.2 3.9 copy.50
  385.6 0.6 copy.80
  386.2 3.6 all-to-all-start.3
  389.9 0.7 all-gather.11.cloned.1.call-update
  390.6 0.6 copy.81
  391.2 2.9 copy.56
  394.2 2.4 all-to-all-done.3
  396.5 3.7 all-to-all-start.1
  400.2 2.9 convolution_bitcast_fusion
  403.1 3.7 copy.57
  406.7 0.3 all-to-all-done.1
  407.0 5.7 all-to-all-start.2
  413.0 36.6 %while.14 = (s32[]{:T(128)}, f32[2,1024,4,128]{1,3,2,0:T(8,128)}, f32[2,1024,4]{1,2,0:T(4,128)S(1)}, f32[2,1024,4]{1,2,0:T(4,128)S(1)}, bf16[2,1024,4,384]{3,2,1,0:T(4,128)(2,1)}, /*index=5*/s32[]{:T(128)}) while((s32[]{:T(128)}, f32[2,1024,4,128]{1,3,2,0:T(8,128)}, f32[2,1024,4]{1,2,0:T(4,128)S(1)}, f32[2,1024,4]{1,2,0:T(4,128)S(1)}, ...), condition=%wide.region_5.6_spmd, body=%wide.region_2.5_spmd.sunk | while | flops 2203049984 | bytes 85065848 | solution.py:80
  413.0 0.3 iota_compare_fusion.3
  413.4 3.0 constant_dynamic-slice_fusion.2
  416.3 0.4 copy.83
  416.8 3.2 fusion.49
  419.9 4.2 fusion.50
  424.1 7.2 %bitcast_dynamic-update-slice_fusion.5 = f32[2,1024,4,128]{1,3,2,0:T(8,128)} fusion(f32[2,1024,4,128]{1,3,2,0:T(8,128)} %get-tuple-element.130, s32[]{:T(128)S(6)} %copy.91, f32[4,1024,1024]{1,2,0:T(8,128)S(1)} %get-tuple-element.119, f32[4,1024]{1,0:T(4,128)S(1)} %get-tuple-element.120, pred[1024,1024]{0,1:T(8,128)(4,1)S(1)} %iota_compare_fusion.3, ...), kind=kOutput, calls=%fused_computation.9.clone.1 | convolution fusion | flops 1094713344 | bytes 20987908 | tf_op jit(solution)/shard_map/while/body/eval_jaxpr/hce,ehd->chd/dot_general | solution.py:31
  431.3 0.3 iota_compare_fusion.3
  431.6 3.0 constant_dynamic-slice_fusion.2
  434.6 0.4 copy.83
  435.0 3.2 fusion.49
  438.2 4.2 fusion.50
  442.4 7.2 %bitcast_dynamic-update-slice_fusion.5 = f32[2,1024,4,128]{1,3,2,0:T(8,128)} fusion(f32[2,1024,4,128]{1,3,2,0:T(8,128)} %get-tuple-element.130, s32[]{:T(128)S(6)} %copy.91, f32[4,1024,1024]{1,2,0:T(8,128)S(1)} %get-tuple-element.119, f32[4,1024]{1,0:T(4,128)S(1)} %get-tuple-element.120, pred[1024,1024]{0,1:T(8,128)(4,1)S(1)} %iota_compare_fusion.3, ...), kind=kOutput, calls=%fused_computation.9.clone.1 | convolution fusion | flops 1094713344 | bytes 20987908 | tf_op jit(solution)/shard_map/while/body/eval_jaxpr/hce,ehd->chd/dot_general | solution.py:31
  449.7 73.1 %all-to-all-done.2 = f32[16,128,4,128]{3,2,1,0:T(4,128)} async-done(((f32[16,128,4,128]{3,2,1,0:T(4,128)}), f32[16,128,4,128]{3,2,1,0:T(4,128)}, u32[]{:S(2)}, u32[]{:S(2)}) %all-to-all-start.2) | async-done | bytes 4194336 | tf_op jit(solution)/shard_map/all_to_all | solution.py:59
  522.8 4.3 copy.58
  527.0 4.9 all_to_all.63
  531.9 4.6 divide_convert_fusion
  536.6 2.5 copy.63
  539.1 3.5 copy.79
  542.6 57.8 %all-gather.9.cloned.1.call-done = bf16[2048,2048]{1,0:T(8,128)(2,1)} async-done(((bf16[2048,512]{1,0:T(8,128)(2,1)}), bf16[2048,2048]{1,0:T(8,128)(2,1)}) %all-gather.9.cloned.1.call-update) | async-done | bytes 8388624 | tf_op jit(solution)/shard_map/all_gather | solution.py:94
  600.4 9.8 %add_convert_fusion = bf16[2048,512]{1,0:T(8,128)(2,1)} fusion(bf16[2048,512]{1,0:T(8,128)(2,1)S(1)} %copy-done.2, bf16[2048,2048]{1,0:T(8,128)(2,1)} %all-gather.9.cloned.1.call-done, bf16[2048,512]{1,0:T(8,128)(2,1)} %all-gather.11.cloned.1.call-done), kind=kOutput, calls=%fused_computation.33 | convolution fusion | flops 4298113024 | bytes 14680064 | tf_op jit(solution)/shard_map/dot_general | solution.py:93
  (32 shorter events, 1.0 us)
Async XLA Ops:
  6.5 63.4 %all-gather.5.cloned.1.call-start = ((), (), s32[]{:S(2)}) async-start(), calls=%async_computation.4 | async-start | bytes 10485760 | tf_op jit(solution)/shard_map/all_gather | solution.py:67
  7.3 163.9 %all-gather.7.cloned.1.call-start = ((), (), s32[]{:S(2)}) async-start(), calls=%async_computation.5 | async-start | bytes 7077888 | tf_op jit(solution)/shard_map/all_gather | solution.py:73
  69.9 5.8 copy-start.1
  74.6 96.6 %copy-start.3 = (f32[2048]{0:T(1024)S(1)}, f32[2048]{0:T(1024)}, u32[]{:S(2)}) copy-start(f32[2048]{0:T(1024)} %param.7) | copy-start | bytes 24580
  209.2 142.7 %all-to-all-start = ((bf16[2,1024,4,384]{3,2,0,1:T(4,128)(2,1)}), bf16[2,1024,4,384]{3,2,0,1:T(4,128)(2,1)}, u32[]{:S(2)}, u32[]{:S(2)}) async-start(bf16[2,1024,4,384]{3,2,0,1:T(4,128)(2,1)} %copy.48), calls=%async_computation | async-start | bytes 12582912 | tf_op jit(solution)/shard_map/all_to_all | solution.py:82
  386.2 10.3 %all-to-all-start.3 = ((f32[16,128,4]{1,2,0:T(4,128)}), f32[16,128,4]{1,2,0:T(4,128)S(1)}, u32[]{:S(2)}, u32[]{:S(2)}) async-start(f32[16,128,4]{1,2,0:T(4,128)} %bitcast.59), calls=%async_computation.3 | async-start | bytes 65536 | tf_op jit(solution)/shard_map/all_to_all | solution.py:61
  389.8 152.8 %all-gather.11.cloned.1.call-start = ((), (), s32[]{:S(2)}) async-start(), calls=%async_computation.7 | async-start | bytes 2359296 | tf_op jit(solution)/shard_map/all_gather | solution.py:74
  396.5 10.5 %all-to-all-start.1 = ((f32[16,128,4]{1,2,0:T(4,128)}), f32[16,128,4]{1,2,0:T(4,128)S(1)}, u32[]{:S(2)}, u32[]{:S(2)}) async-start(f32[16,128,4]{1,2,0:T(4,128)} %bitcast.60), calls=%async_computation.1 | async-start | bytes 65536 | tf_op jit(solution)/shard_map/all_to_all | solution.py:60
  407.0 115.8 %all-to-all-start.2 = ((f32[16,128,4,128]{3,2,1,0:T(4,128)}), f32[16,128,4,128]{3,2,1,0:T(4,128)}, u32[]{:S(2)}, u32[]{:S(2)}) async-start(f32[16,128,4,128]{3,2,1,0:T(4,128)} %copy.57), calls=%async_computation.2 | async-start | bytes 8388608 | tf_op jit(solution)/shard_map/all_to_all | solution.py:59
  412.8 187.7 %all-gather.9.cloned.1.call-start = ((), (), s32[]{:S(2)}) async-start(), calls=%async_computation.6 | async-start | bytes 10485760 | tf_op jit(solution)/shard_map/all_gather | solution.py:94
  416.7 3.2 copy-start
  435.0 3.2 copy-start
  539.1 61.3 %copy-start.2 = (bf16[2048,512]{1,0:T(8,128)(2,1)S(1)}, bf16[2048,512]{1,0:T(8,128)(2,1)}, u32[]{:S(2)}) copy-start(bf16[2048,512]{1,0:T(8,128)(2,1)} %param.6) | copy-start | bytes 6291460
Sparse Core Ops, SparseCore 0:
  8.9 60.9 all-gather.4
  72.1 99.0 all-gather.6
  392.8 113.3 all-gather.10
  542.7 57.6 all-gather.8
where the time goes:
time: 618 us; the launch traced here: 617 us
  waiting for transfers between devices  428 us (69%)
  local copies, waits for them, and re-layouts  77.7 us (13%)
  matrix products  57.8 us (9%)
  other arithmetic  21.1 us (3%)
  starting transfers between devices  18.3 us (3%)
  between operations  13.3 us (2%)
    all_to_all x1, waiting for transfers between devices, per_device(): lax.all_to_all(stacked, 'row', split_axis=1, concat_axis=0, tiled=True)  138 us
    all_gather x1, waiting for transfers between devices, per_device(): piece_qkv = lax.all_gather(qkv_weight, 'row', axis=0, tiled=True)  93.2 us
    all_to_all x1, waiting for transfers between devices, column_softmax(): lax.all_to_all(summed, 'row', split_axis=0, concat_axis=1, tiled=True)  73.1 us
    all_gather x1, waiting for transfers between devices, per_device(): gathered = lax.all_gather(signal, 'col', axis=1, tiled=True)  61.9 us
    all_gather x1, waiting for transfers between devices, per_device(): lax.all_gather(attended, 'col', axis=1, tiled=True)  57.8 us
    all_to_all x2, local copies, waits for them, and re-layouts, per_device(): lax.all_to_all(stacked, 'row', split_axis=1, concat_axis=0, tiled=True)  24 us
    dot_general x1, matrix products, per_device(): jnp.dot(normed, piece_qkv, preferred_element_type=jnp.float32)  19.1 us
    reshape x2, local copies, waits for them, and re-layouts, per_device(): stacked = qkv.reshape(rows_here, COLS, heads_here, 3 * HS)  18.9 us
  transfers between devices with their start and end apart: 8, of which 7 were waited for; matrix products, arithmetic and copies ran while one was open for 11% of the time, Pallas kernels for 0%

commit v1 on v0

v1 whole, which is shorter than its diff:
```python
import functools
import math

import jax
import jax.numpy as jnp
from jax import lax
from jax.experimental import pallas as pl
from jax.experimental.pallas import tpu as pltpu
from jax.sharding import PartitionSpec as P

HS = 128
COLS = 1024
GROUP = 16
LANES = 128

EPSILON = 1e-05
NEGATIVE = -1e30
VMEM_LIMIT = 56 * 1024 * 1024
F32 = jnp.float32
BF16 = jnp.bfloat16


def block_of(size, most):
    while size % most:
        most //= 2
    return most


def norm_project_kernel(sig_ref, gain_ref, weight_ref, out_ref):
    pieces, _, width = sig_ref.shape
    parts = [sig_ref[i].astype(F32) for i in range(pieces)]
    total = sum(jnp.sum(part, axis=1, keepdims=True) for part in parts)
    average = total / (pieces * width)
    parts = [part - average for part in parts]
    squares = sum(jnp.sum(part * part, axis=1, keepdims=True) for part in parts)
    scale = lax.rsqrt(squares / (pieces * width) + EPSILON)
    normed = jnp.concatenate(
        [
            (part * scale * gain_ref[:, i * width : (i + 1) * width]).astype(BF16)
            for i, part in enumerate(parts)
        ],
        axis=1,
    )
    out_ref[...] = jnp.dot(normed, weight_ref[...], preferred_element_type=F32).astype(BF16)


def norm_project(gathered, norm_gain, weight):
    pieces, tokens, width = gathered.shape
    features, outs = weight.shape
    block = block_of(tokens, 256)
    return pl.pallas_call(
        norm_project_kernel,
        out_shape=jax.ShapeDtypeStruct((tokens, outs), BF16),
        grid=(tokens // block,),
        in_specs=[
            pl.BlockSpec((pieces, block, width), lambda i: (0, i, 0)),
            pl.BlockSpec((1, features), lambda i: (0, 0)),
            pl.BlockSpec((features, outs), lambda i: (0, 0)),
        ],
        out_specs=pl.BlockSpec((block, outs), lambda i: (i, 0)),
        compiler_params=pltpu.CompilerParams(vmem_limit_bytes=VMEM_LIMIT),
        cost_estimate=pl.CostEstimate(
            flops=2 * tokens * features * outs,
            bytes_accessed=2 * (tokens * features + features * outs + tokens * outs),
            transcendentals=0,
        ),
    )(gathered, norm_gain.reshape(1, features), weight)


def softmax_part(queries, keys, values, allowed):
    factor = 1.0 / math.sqrt(HS)
    scores = lax.dot_general(
        queries, keys, (((1,), (1,)), ((), ())), preferred_element_type=F32
    )
    if allowed is not None:
        first = scores.shape[1] - allowed.shape[1]
        tail = jnp.where(allowed, scores[:, first:], NEGATIVE)
        scores = tail if first == 0 else jnp.concatenate([scores[:, :first], tail], axis=1)
    top = jnp.max(scores, axis=1, keepdims=True)
    weights = jnp.exp2((scores - top) * (factor * math.log2(math.e)))
    return scores, top, weights, factor


def row_kernel(qkv_ref, acc_ref, stat_ref, *, heads, block):
    length = qkv_ref.shape[0]
    line = lax.broadcasted_iota(jnp.int32, (block, block), 0)
    lane = lax.broadcasted_iota(jnp.int32, (block, block), 1)
    allowed = line >= lane
    place = lax.broadcasted_iota(jnp.int32, (block, LANES), 1)
    for part in range(length // block):
        rows = slice(part * block, (part + 1) * block)
        reach = slice(0, (part + 1) * block)
        stats = jnp.zeros((block, LANES), F32)
        for head in range(heads):
            at = head * 3 * HS
            _, top, weights, factor = softmax_part(
                qkv_ref[rows, at : at + HS],
                qkv_ref[reach, at + HS : at + 2 * HS],
                None,
                allowed,
            )
            total = jnp.sum(weights, axis=1, keepdims=True)
            summed = jnp.dot(
                weights.astype(BF16),
                qkv_ref[reach, at + 2 * HS : at + 3 * HS],
                preferred_element_type=F32,
            )
            acc_ref[rows, head * HS : (head + 1) * HS] = summed
            stats = jnp.where(place == head, top * factor, stats)
            stats = jnp.where(place == heads + head, total, stats)
        stat_ref[rows, :] = stats


def row_attention(qkv, heads):
    tokens, width = qkv.shape
    return pl.pallas_call(
        functools.partial(row_kernel, heads=heads, block=block_of(COLS, 256)),
        out_shape=(
            jax.ShapeDtypeStruct((tokens, heads * HS), F32),
            jax.ShapeDtypeStruct((tokens, LANES), F32),
        ),
        grid=(tokens // COLS,),
        in_specs=[pl.BlockSpec((COLS, width), lambda i: (i, 0))],
        out_specs=(
            pl.BlockSpec((COLS, heads * HS), lambda i: (i, 0)),
            pl.BlockSpec((COLS, LANES), lambda i: (i, 0)),
        ),
        compiler_params=pltpu.CompilerParams(vmem_limit_bytes=VMEM_LIMIT),
        cost_estimate=pl.CostEstimate(
            flops=4 * tokens * COLS * heads * HS,
            bytes_accessed=2 * tokens * width + 4 * tokens * heads * HS,
            transcendentals=tokens * COLS * heads,
        ),
    )(qkv)


def column_kernel(qkv_ref, mean_ref, stat_ref, *, heads):
    lines = qkv_ref.shape[0]
    count = lines * GROUP
    line = lax.broadcasted_iota(jnp.int32, (count, count), 0)
    lane = lax.broadcasted_iota(jnp.int32, (count, count), 1)
    allowed = jnp.logical_and(
        lax.rem(line, GROUP) == lax.rem(lane, GROUP), line // GROUP > lane // GROUP
    )
    place = lax.broadcasted_iota(jnp.int32, (count, LANES), 1)
    some = lax.broadcasted_iota(jnp.int32, (count, 1), 0) >= GROUP
    stats = jnp.zeros((count, LANES), F32)
    for head in range(heads):
        at = head * 3 * HS
        queries, keys, values = (
            qkv_ref[:, :, at + i * HS : at + (i + 1) * HS].reshape(count, HS) for i in range(3)
        )
        _, top, weights, factor = softmax_part(queries, keys, None, allowed)
        weights = jnp.where(allowed, weights, 0.0)
        total = jnp.sum(weights, axis=1, keepdims=True)
        summed = jnp.dot(weights.astype(BF16), values, preferred_element_type=F32)
        mean = jnp.where(some, summed / jnp.where(some, total, 1.0), 0.0)
        mean_ref[:, :, head * HS : (head + 1) * HS] = mean.astype(BF16).reshape(
            lines, GROUP, HS
        )
        stats = jnp.where(place == head, jnp.where(some, top * factor, NEGATIVE), stats)
        stats = jnp.where(place == heads + head, total, stats)
    stat_ref[0] = stats.T[: stat_ref.shape[1], :]


def column_attention(qkv, heads, held):
    lines, columns, width = qkv.shape
    groups = columns // GROUP
    return pl.pallas_call(
        functools.partial(column_kernel, heads=heads),
        out_shape=(
            jax.ShapeDtypeStruct((lines, columns, heads * HS), BF16),
            jax.ShapeDtypeStruct((groups, held, lines * GROUP), F32),
        ),
        grid=(groups,),
        in_specs=[pl.BlockSpec((lines, GROUP, width), lambda i: (0, i, 0))],
        out_specs=(
            pl.BlockSpec((lines, GROUP, heads * HS), lambda i: (0, i, 0)),
            pl.BlockSpec((1, held, lines * GROUP), lambda i: (i, 0, 0)),
        ),
        compiler_params=pltpu.CompilerParams(vmem_limit_bytes=VMEM_LIMIT),
    )(qkv)


def merge_kernel(acc_ref, rstat_ref, mean_ref, cstat_ref, out_ref, *, heads):
    rstat = rstat_ref[...]
    held, block = cstat_ref.shape[1:]
    cstat = cstat_ref[0]
    if held < LANES:
        cstat = jnp.concatenate([cstat, jnp.zeros((LANES - held, block), F32)], axis=0)
    cstat = cstat.T
    sources, _, columns, _ = mean_ref.shape
    for head in range(heads):
        across = slice(head * HS, (head + 1) * HS)
        row_max = rstat[:, head : head + 1]
        row_total = rstat[:, heads + head : heads + head + 1]
        col_max = cstat[:, head : head + 1]
        col_total = cstat[:, heads + head : heads + head + 1]
        top = jnp.maximum(row_max, col_max)
        row_factor = jnp.exp(row_max - top)
        col_part = jnp.exp(col_max - top) * col_total
        share = 1.0 / (row_factor * row_total + col_part)
        mean = mean_ref[:, 0, :, across].reshape(sources * columns, HS).astype(F32)
        out_ref[:, across] = (
            (row_factor * share) * acc_ref[:, across] + (col_part * share) * mean
        ).astype(BF16)


def merge(row_acc, row_stats, col_mean, col_stats, heads):
    tokens, width = row_acc.shape
    sources, _, columns, _ = col_mean.shape
    held = col_stats.shape[1]
    return pl.pallas_call(
        functools.partial(merge_kernel, heads=heads),
        out_shape=jax.ShapeDtypeStruct((tokens, width), BF16),
        grid=(tokens // COLS,),
        in_specs=[
            pl.BlockSpec((COLS, width), lambda i: (i, 0)),
            pl.BlockSpec((COLS, LANES), lambda i: (i, 0)),
            pl.BlockSpec((sources, 1, columns, width), lambda i: (0, i, 0, 0)),
            pl.BlockSpec((1, held, COLS), lambda i: (i, 0, 0)),
        ],
        out_specs=pl.BlockSpec((COLS, width), lambda i: (i, 0)),
        compiler_params=pltpu.CompilerParams(vmem_limit_bytes=VMEM_LIMIT),
    )(row_acc, row_stats, col_mean, col_stats)


def project_kernel(att_ref, weight_ref, signal_ref, out_ref):
    pieces, _, width = att_ref.shape
    joined = jnp.concatenate([att_ref[i] for i in range(pieces)], axis=1)
    branch = jnp.dot(joined, weight_ref[...], preferred_element_type=F32)
    out_ref[...] = (signal_ref[...].astype(F32) + branch).astype(BF16)


def project(gathered, weight, signal):
    pieces, tokens, width = gathered.shape
    features, outs = weight.shape
    block = block_of(tokens, 256)
    return pl.pallas_call(
        project_kernel,
        out_shape=jax.ShapeDtypeStruct((tokens, outs), BF16),
        grid=(tokens // block,),
        in_specs=[
            pl.BlockSpec((pieces, block, width), lambda i: (0, i, 0)),
            pl.BlockSpec((features, outs), lambda i: (0, 0)),
            pl.BlockSpec((block, outs), lambda i: (i, 0)),
        ],
        out_specs=pl.BlockSpec((block, outs), lambda i: (i, 0)),
        compiler_params=pltpu.CompilerParams(vmem_limit_bytes=VMEM_LIMIT),
    )(gathered, weight, signal)


def per_device(signal, norm_gain, qkv_weight, out_weight):
    samples, width = signal.shape
    count = lax.axis_size("row")
    rows_here = samples // COLS
    lines = rows_here * count
    columns = COLS // count
    heads = qkv_weight.shape[1] // (3 * HS)
    held = -(-2 * heads // 8) * 8

    spread = jnp.transpose(signal.reshape(rows_here, count, columns, width), (1, 0, 2, 3))
    crossed = lax.all_to_all(spread, "row", split_axis=0, concat_axis=0, tiled=True)
    crossed = crossed.reshape(lines * columns, width)
    piece_qkv = lax.all_gather(qkv_weight, "row", axis=0, tiled=True)
    col_signal = lax.all_gather(crossed, "col", axis=0)
    row_signal = lax.all_gather(signal, "col", axis=0)
    piece_out = lax.all_gather(out_weight, "row", axis=0, tiled=True)

    col_qkv = norm_project(col_signal, norm_gain, piece_qkv)
    col_mean, col_stats = column_attention(
        col_qkv.reshape(lines, columns, 3 * heads * HS), heads, held
    )
    col_stats = jnp.transpose(
        col_stats.reshape(columns // GROUP, held, lines, GROUP), (2, 1, 0, 3)
    ).reshape(lines, held, columns)
    col_stats = lax.all_to_all(col_stats, "row", split_axis=0, concat_axis=2, tiled=True)
    col_mean = lax.all_to_all(
        col_mean.reshape(count, rows_here, columns, heads * HS),
        "row",
        split_axis=0,
        concat_axis=0,
        tiled=True,
    )
    row_qkv = norm_project(row_signal, norm_gain, piece_qkv)
    row_acc, row_stats = row_attention(row_qkv, heads)
    attended = merge(row_acc, row_stats, col_mean, col_stats, heads)
    return project(lax.all_gather(attended, "col", axis=0), piece_out, signal)


def solution(mesh):
    return jax.shard_map(
        per_device,
        mesh=mesh,
        in_specs=(P("row", "col"), P(), P("row", "col"), P("row", "col")),
        out_specs=P("row", "col"),
        check_vma=False,
    )
```

time: 618 us -> 404 us (0.65)
  waiting for transfers between devices: 428 us -> 201 us
  blocking collectives: 0 us -> 93 us
  Pallas kernels: 0 us -> 86.8 us
  local copies, waits for them, and re-layouts: 77.7 us -> 5.26 us
  matrix products: 57.8 us -> 0 us
  other arithmetic: 21.1 us -> 0 us
  starting transfers between devices: 18.3 us -> 3.95 us
    all_to_all x4 -> x1, waiting for transfers between devices: 213 us -> 7.83 us  [per_device(): lax.all_to_all(col_mean.reshape(count, rows_here, columns, heads * HS), '...]
    all_to_all x0 -> x2, blocking collectives: none -> 93 us  [the longest x1 80.8 us: per_device(): lax.all_to_all(spread, 'row', split_axis=0, concat_axis=0, tiled=True)]
    pallas_call x0 -> x6, Pallas kernels: none -> 86.8 us  [the longest x2 44.8 us: norm_project(): pl.pallas_call(norm_project_kernel, out_shape=jax.ShapeDtypeStruct((token...]
    dot_general x8 -> x0, matrix products: 57.8 us -> none  [the longest x1 19.1 us: per_device(): jnp.dot(normed, piece_qkv, preferred_element_type=jnp.float32)]
    all_gather x1, waiting for transfers between devices: 93.2 us -> 52.6 us  [per_device(): piece_qkv = lax.all_gather(qkv_weight, 'row', axis=0, tiled=True)]
    all_to_all x10 -> x1, local copies, waits for them, and re-layouts: 33.2 us -> 0.62 us  [per_device(): lax.all_to_all(col_stats, 'row', split_axis=0, concat_axis=2, tiled=True)]
    reduce_sum x5 -> x0, other arithmetic: 15.7 us -> none  [the longest x2 8.38 us: row_softmax(): totals = jnp.sum(weights, axis=-1)]
    reshape x2 -> x4, local copies, waits for them, and re-layouts: 18.9 us -> 3.32 us  [the longest x1 1.79 us: per_device(): signal.reshape(rows_here, count, columns, width)]
  transfers between devices with their start and end apart: 8 -> 6, of which waited for: 7 -> 6; matrix products, arithmetic and copies ran while one was open for 11% -> 1% of each run, Pallas kernels for 0% -> 19%
where the time goes in v1:
time: 404 us
  waiting for transfers between devices  201 us (50%)
  blocking collectives  93 us (23%)
  Pallas kernels  86.8 us (21%)
  between operations  13.2 us (3%)
  local copies, waits for them, and re-layouts  5.26 us (1%)
    all_to_all x1, blocking collectives, per_device(): lax.all_to_all(spread, 'row', split_axis=0, concat_axis=0, tiled=True)  80.8 us
    all_gather x1, waiting for transfers between devices, per_device(): col_signal = lax.all_gather(crossed, 'col', axis=0)  58.5 us
    all_gather x1, waiting for transfers between devices, per_device(): return project(lax.all_gather(attended, 'col', axis=0), piece_out, signal)  58.2 us
    all_gather x1, waiting for transfers between devices, per_device(): piece_qkv = lax.all_gather(qkv_weight, 'row', axis=0, tiled=True)  52.6 us
    pallas_call x2, Pallas kernels, norm_project(): pl.pallas_call(norm_project_kernel, out_shape=jax.ShapeDtypeStruct((token...  44.8 us
    pallas_call x1, Pallas kernels, row_attention(): pl.pallas_call(functools.partial(row_kernel, heads=heads, block=block_of(...  15 us
    all_gather x1, waiting for transfers between devices, per_device(): piece_out = lax.all_gather(out_weight, 'row', axis=0, tiled=True)  13.1 us
    all_to_all x1, blocking collectives, per_device(): lax.all_to_all(col_stats, 'row', split_axis=0, concat_axis=2, tiled=True)  12.2 us
  transfers between devices with their start and end apart: 6, of which 6 were waited for; matrix products, arithmetic and copies ran while one was open for 1% of the time, Pallas kernels for 19%

profile of v1, /device:TPU:0, one launch (start us, length us, event | category | flops | bytes accessed | tf_op | source)
XLA Modules:
  0.0 403.6 jit_solution(5373327563039039832)
XLA Ops:
  6.5 0.0 all-gather.8.cloned.1.call-start
  6.5 0.7 all-gather.8.cloned.1.call-update
  7.3 0.0 all-gather.10.cloned.1.call-start
  7.3 1.8 copy.15
  9.1 80.8 %all_to_all.28 = bf16[8,2,128,512]{3,2,1,0:T(8,128)(2,1)} all-to-all(bf16[8,2,128,512]{3,2,1,0:T(8,128)(2,1)S(1)} %bitcast.24), channel_id=1, replica_groups=mesh['row'=8,'col'=4] {'row'}, dimensions={0} | all-to-all | bytes 4194304 | tf_op jit(solution)/shard_map/all_to_all | solution.py:263
  89.9 0.0 all-gather.10.cloned.1.call-update
  89.9 0.0 all-gather.14.cloned.1.call-start
  90.0 0.7 all-gather.14.cloned.1.call-update
  90.7 52.6 %all-gather.8.cloned.1.call-done.weight_ref = bf16[2048,1536]{1,0:T(8,128)(2,1)} async-done(((bf16[256,1536]{1,0:T(8,128)(2,1)}), bf16[2048,1536]{1,0:T(8,128)(2,1)}) %all-gather.8.cloned.1.call-update) | async-done | bytes 6291472 | tf_op jit(solution)/shard_map/all_gather | solution.py:265
  143.3 58.5 %all-gather.10.cloned.1.call-done.sig_ref = bf16[4,2048,512]{2,1,0:T(8,128)(2,1)} async-done(((bf16[1,2048,512]{2,1,0:T(8,128)(2,1)}), bf16[4,2048,512]{2,1,0:T(8,128)(2,1)}) %all-gather.10.cloned.1.call-update) | async-done | bytes 8388624 | tf_op jit(solution)/shard_map/all_gather | solution.py:266
  201.8 22.4 %shard_map.48 = bf16[2048,1536]{1,0:T(8,128)(2,1)} custom-call(bf16[4,2048,512]{2,1,0:T(8,128)(2,1)} %all-gather.10.cloned.1.call-done.sig_ref, f32[1,2048]{1,0:T(1,128)} %bitcast.31, bf16[2048,1536]{1,0:T(8,128)(2,1)} %all-gather.8.cloned.1.call-done.weight_ref), custom_call_target="tpu_custom_call" | custom-call | flops 12884901888 | bytes 20971520 | tf_op jit(solution)/shard_map/pallas_call | solution.py:51
  224.2 10.1 %shard_map.49 = (bf16[16,128,512]{2,1,0:T(8,128)(2,1)}, f32[8,8,256]{2,1,0:T(8,128)}) custom-call(bf16[16,128,1536]{2,1,0:T(8,128)(2,1)} %bitcast.25), custom_call_target="tpu_custom_call" | custom-call | tf_op jit(solution)/shard_map/pallas_call | solution.py:169
  234.3 1.0 reshape.23
  235.3 0.3 copy.16
  235.6 0.2 reshape.24
  235.8 12.2 %all_to_all.29 = f32[16,8,128]{2,1,0:T(8,128)S(1)} all-to-all(f32[16,8,128]{2,1,0:T(8,128)S(1)} %reshape.24), channel_id=1, replica_groups=mesh['row'=8,'col'=4] {'row'}, dimensions={0} | all-to-all | bytes 131072 | tf_op jit(solution)/shard_map/all_to_all | solution.py:277
  248.0 3.6 all-to-all-start.1
  251.7 0.0 all-gather.12.cloned.1.call-start
  251.7 0.5 all-gather.12.cloned.1.call-update
  252.2 0.2 all-gather.16.cloned.1.call-start
  252.5 9.2 %all-gather.14.cloned.1.call-done = bf16[8192,512]{1,0:T(8,128)(2,1)} async-done(((bf16[2048,512]{1,0:T(8,128)(2,1)}), bf16[8192,512]{1,0:T(8,128)(2,1)}) %all-gather.14.cloned.1.call-update) | async-done | bytes 8388624 | tf_op jit(solution)/shard_map/all_gather | solution.py:267
  261.7 22.4 %shard_map.46.qkv_ref = bf16[2048,1536]{1,0:T(8,128)(2,1)} custom-call(bf16[4,2048,512]{2,1,0:T(8,128)(2,1)} %bitcast.30, f32[1,2048]{1,0:T(1,128)} %bitcast.32, bf16[2048,1536]{1,0:T(8,128)(2,1)} %all-gather.8.cloned.1.call-done.weight_ref), custom_call_target="tpu_custom_call" | custom-call | flops 12884901888 | bytes 20971520 | tf_op jit(solution)/shard_map/pallas_call | solution.py:51
  284.1 15.0 %shard_map.47 = (f32[2048,512]{1,0:T(8,128)}, f32[2048,128]{1,0:T(8,128)}) custom-call(bf16[2048,1536]{1,0:T(8,128)(2,1)} %shard_map.46.qkv_ref), custom_call_target="tpu_custom_call" | custom-call | flops 4294967296 | bytes 10485760 | tf_op jit(solution)/shard_map/pallas_call | solution.py:116
  299.1 0.6 copy.17
  299.7 7.8 %all-to-all-done.1.mean_ref = bf16[8,2,128,512]{3,2,1,0:T(8,128)(2,1)S(1)} async-done(((bf16[8,2,128,512]{3,2,1,0:T(8,128)(2,1)}), bf16[8,2,128,512]{3,2,1,0:T(8,128)(2,1)S(1)}, u32[]{:S(2)}, u32[]{:S(2)}) %all-to-all-start.1) | async-done | bytes 2097184 | tf_op jit(solution)/shard_map/all_to_all | solution.py:278
  307.5 0.0 copy-start
  307.5 1.3 copy-done
  308.8 6.2 %shard_map.50 = bf16[2048,512]{1,0:T(8,128)(2,1)} custom-call(f32[2048,512]{1,0:T(8,128)} %get-tuple-element.9.acc_ref, f32[2048,128]{1,0:T(8,128)} %get-tuple-element.10.rstat_ref, bf16[8,2,128,512]{3,2,1,0:T(8,128)(2,1)} %copy-done, f32[2,8,1024]{2,1,0:T(8,128)} %bitcast.28), custom_call_target="tpu_custom_call" | custom-call | tf_op jit(solution)/shard_map/pallas_call | solution.py:213
  315.1 0.0 all-gather.16.cloned.1.call-update
  315.1 13.1 %all-gather.12.cloned.1.call-done.weight_ref = bf16[2048,512]{1,0:T(8,128)(2,1)} async-done(((bf16[256,512]{1,0:T(8,128)(2,1)}), bf16[2048,512]{1,0:T(8,128)(2,1)}) %all-gather.12.cloned.1.call-update) | async-done | bytes 2097168 | tf_op jit(solution)/shard_map/all_gather | solution.py:268
  328.2 58.2 %all-gather.16.cloned.1.call-done = bf16[8192,512]{1,0:T(8,128)(2,1)} async-done(((bf16[2048,512]{1,0:T(8,128)(2,1)}), bf16[8192,512]{1,0:T(8,128)(2,1)}) %all-gather.16.cloned.1.call-update) | async-done | bytes 8388624 | tf_op jit(solution)/shard_map/all_gather | solution.py:288
  386.4 10.7 %shard_map.51 = bf16[2048,512]{1,0:T(8,128)(2,1)} custom-call(bf16[4,2048,512]{2,1,0:T(8,128)(2,1)} %bitcast.22, bf16[2048,512]{1,0:T(8,128)(2,1)} %all-gather.12.cloned.1.call-done.weight_ref, bf16[2048,512]{1,0:T(8,128)(2,1)} %signal_ref.1), custom_call_target="tpu_custom_call" | custom-call | tf_op jit(solution)/shard_map/pallas_call | solution.py:239
Async XLA Ops:
  6.5 136.8 %all-gather.8.cloned.1.call-start = ((), (), s32[]{:S(2)}) async-start(), calls=%async_computation.3 | async-start | bytes 7077888 | tf_op jit(solution)/shard_map/all_gather | solution.py:265
  7.3 194.5 %all-gather.10.cloned.1.call-start = ((), (), s32[]{:S(2)}) async-start(), calls=%async_computation.4 | async-start | bytes 10485760 | tf_op jit(solution)/shard_map/all_gather | solution.py:266
  89.9 171.8 %all-gather.14.cloned.1.call-start = ((), (), s32[]{:S(2)}) async-start(), calls=%async_computation.6 | async-start | bytes 10485760 | tf_op jit(solution)/shard_map/all_gather | solution.py:267
  248.0 59.5 %all-to-all-start.1 = ((bf16[8,2,128,512]{3,2,1,0:T(8,128)(2,1)}), bf16[8,2,128,512]{3,2,1,0:T(8,128)(2,1)S(1)}, u32[]{:S(2)}, u32[]{:S(2)}) async-start(bf16[8,2,128,512]{3,2,1,0:T(8,128)(2,1)} %bitcast.26), calls=%async_computation.1 | async-start | bytes 4194304 | tf_op jit(solution)/shard_map/all_to_all | solution.py:278
  251.7 76.5 %all-gather.12.cloned.1.call-start = ((), (), s32[]{:S(2)}) async-start(), calls=%async_computation.5 | async-start | bytes 2359296 | tf_op jit(solution)/shard_map/all_gather | solution.py:268
  252.2 134.2 %all-gather.16.cloned.1.call-start = ((), (), s32[]{:S(2)}) async-start(), calls=%async_computation.7 | async-start | bytes 10485760 | tf_op jit(solution)/shard_map/all_gather | solution.py:288
  307.5 1.3 copy-start
Sparse Core Ops, SparseCore 0:
  9.5 133.7 all-gather.7
  144.8 56.8 all-gather.9
  203.3 58.2 all-gather.13
  263.7 64.4 all-gather.11
  329.6 56.7 all-gather.15

commit v2 on v1

--- a/solution.py
+++ b/solution.py
@@ -250,6 +250,197 @@
     )(gathered, weight, signal)
 
 
+def remote(src, dst, sems, at, target):
+    return pltpu.make_async_remote_copy(
+        src_ref=src,
+        dst_ref=dst,
+        send_sem=sems[0].at[at],
+        recv_sem=sems[1].at[at],
+        device_id=target,
+        device_id_type=pl.DeviceIdType.MESH,
+    )
+
+
+def ring_place(row, half):
+    return (row // 2) * (1 - row % 2) + (2 * half - 1 - row // 2) * (row % 2)
+
+
+def ring_row(place, half):
+    over = place // half
+    return 2 * place * (1 - over) + (2 * (2 * half - 1 - place) + 1) * over
+
+
+def arrive_kernel(
+    signal_ref,
+    weight_ref,
+    crossed_ref,
+    whole_ref,
+    cross_send,
+    cross_recv,
+    peer_send,
+    peer_recv,
+    twin_send,
+    twin_recv,
+    ring_send,
+    ring_recv,
+    local_sem,
+    *,
+    count,
+    pieces,
+):
+    row, col = lax.axis_index("row"), lax.axis_index("col")
+    rows_here = signal_ref.shape[0]
+    depth = weight_ref.shape[0]
+    half = count // 2
+    chips = pieces // 2
+    twin = (row, col + 1 - 2 * (col % 2))
+    peers = [(row, (col + 2 * k) % pieces) for k in range(1, chips)]
+    others = [((row + k) % count, col) for k in range(1, count)]
+
+    barrier = pltpu.get_barrier_semaphore()
+    for target in others + peers + [twin]:
+        pl.semaphore_signal(
+            barrier, inc=1, device_id=target, device_id_type=pl.DeviceIdType.MESH
+        )
+    pl.semaphore_wait(barrier, len(others) + len(peers) + 1)
+
+    def chunk(source_row, source_col):
+        return crossed_ref.at[source_col, pl.ds(source_row * rows_here, rows_here)]
+
+    started = []
+
+    def go(copy):
+        copy.start()
+        started.append(copy)
+        return copy
+
+    own = signal_ref.at[:, row]
+    keep = pltpu.make_async_copy(own, chunk(row, col), local_sem.at[0])
+    keep.start()
+    place = ring_place(row, half)
+    after = (ring_row((place + 1) % count, half), col)
+    before = (ring_row((place + count - 1) % count, half), col)
+
+    def shard(owner, step):
+        if step < half - 1:
+            return [pl.ds(owner * depth, depth)] * 2
+        return [
+            pl.ds(owner * depth, depth // 2),
+            pl.ds(owner * depth + depth // 2, depth // 2),
+        ]
+
+    ring = []
+
+    def ring_step(step):
+        for way, target in ((0, after), (1, before)):
+            offset = count - step if way == 0 else step
+            owner = ring_row((place + offset) % count, half)
+            where = shard(owner, step)[way]
+            if step == 0:
+                source = weight_ref
+                if half == 1:
+                    source = weight_ref.at[pl.ds(way * (depth // 2), depth // 2)]
+            else:
+                source = whole_ref.at[where]
+            ring.append(
+                go(
+                    remote(
+                        source,
+                        whole_ref.at[where],
+                        (ring_send, ring_recv),
+                        2 * step + way,
+                        target,
+                    )
+                )
+            )
+
+    def spread(at, source, source_row):
+        sent = []
+        for j, target in enumerate(peers):
+            sent.append(
+                go(
+                    remote(
+                        source,
+                        chunk(source_row, col),
+                        (peer_send, peer_recv),
+                        at * (chips - 1) + j,
+                        target,
+                    )
+                )
+            )
+        go(remote(source, chunk(source_row, col), (twin_send, twin_recv), at * chips, twin))
+        return sent
+
+    def pass_on(at, sent, source_row):
+        for j, copy in enumerate(sent):
+            copy.wait_recv()
+            piece = chunk(source_row, (col + pieces - 2 * (j + 1)) % pieces)
+            go(remote(piece, piece, (twin_send, twin_recv), at * chips + 1 + j, twin))
+
+    crossing = []
+    for k, target in enumerate(others):
+        crossing.append(
+            go(
+                remote(
+                    signal_ref.at[:, target[0]],
+                    chunk(row, col),
+                    (cross_send, cross_recv),
+                    k,
+                    target,
+                )
+            )
+        )
+    pending = (0, spread(0, own, row), row)
+    ring_step(0)
+    hold = pltpu.make_async_copy(
+        weight_ref, whole_ref.at[pl.ds(row * depth, depth)], local_sem.at[1]
+    )
+    hold.start()
+    step = 1
+    for k in range(1, count):
+        crossing[k - 1].wait_recv()
+        source_row = (row + count - k) % count
+        later = (k, spread(k, chunk(source_row, col), source_row), source_row)
+        pass_on(*pending)
+        pending = later
+        if k % 2 == 0 and step < half:
+            for copy in ring[2 * step - 2 : 2 * step]:
+                copy.wait_recv()
+            ring_step(step)
+            step += 1
+    pass_on(*pending)
+    for copy in ring[2 * half - 2 :]:
+        copy.wait_recv()
+    for at in range(count * chips):
+        remote(own, chunk(row, col), (twin_send, twin_recv), at, twin).wait_recv()
+    for copy in started:
+        copy.wait_send()
+    keep.wait()
+    hold.wait()
+
+
+def arrive(signal, weight, count, pieces):
+    rows_here, _, columns, width = signal.shape
+    depth, outs = weight.shape
+    chips = pieces // 2
+    dma = pltpu.SemaphoreType.DMA
+    sizes = (count - 1, max(1, count * (chips - 1)), count * chips, count)
+    return pl.pallas_call(
+        functools.partial(arrive_kernel, count=count, pieces=pieces),
+        out_shape=(
+            jax.ShapeDtypeStruct((pieces, rows_here * count, columns, width), BF16),
+            jax.ShapeDtypeStruct((depth * count, outs), BF16),
+        ),
+        in_specs=[pl.BlockSpec(memory_space=pl.ANY)] * 2,
+        out_specs=(pl.BlockSpec(memory_space=pl.ANY),) * 2,
+        scratch_shapes=[dma((size,)) for size in sizes for _ in range(2)] + [dma((2,))],
+        compiler_params=pltpu.CompilerParams(collective_id=0, has_side_effects=True),
+        cost_estimate=pl.CostEstimate(
+            flops=0, bytes_accessed=300 * 1024 * 1024, transcendentals=0
+        ),
+    )(signal, weight)
+
+
 def per_device(signal, norm_gain, qkv_weight, out_weight):
     samples, width = signal.shape
     count = lax.axis_size("row")
@@ -259,11 +450,11 @@
     heads = qkv_weight.shape[1] // (3 * HS)
     held = -(-2 * heads // 8) * 8
 
-    spread = jnp.transpose(signal.reshape(rows_here, count, columns, width), (1, 0, 2, 3))
-    crossed = lax.all_to_all(spread, "row", split_axis=0, concat_axis=0, tiled=True)
-    crossed = crossed.reshape(lines * columns, width)
-    piece_qkv = lax.all_gather(qkv_weight, "row", axis=0, tiled=True)
-    col_signal = lax.all_gather(crossed, "col", axis=0)
+    pieces = lax.axis_size("col")
+    col_signal, piece_qkv = arrive(
+        signal.reshape(rows_here, count, columns, width), qkv_weight, count, pieces
+    )
+    col_signal = col_signal.reshape(pieces, lines * columns, width)
     row_signal = lax.all_gather(signal, "col", axis=0)
     piece_out = lax.all_gather(out_weight, "row", axis=0, tiled=True)
 

time: 404 us -> 320 us (0.79)
  Pallas kernels: 86.8 us -> 203 us
  waiting for transfers between devices: 201 us -> 85.7 us
  blocking collectives: 93 us -> 10.4 us
    pallas_call x0 -> x1, Pallas kernels: none -> 116 us  [arrive(): pl.pallas_call(functools.partial(arrive_kernel, count=count, pieces=piece...]
    all_gather x2 -> x0, waiting for transfers between devices: 111 us -> none  [the longest x1 58.5 us: per_device(): col_signal = lax.all_gather(crossed, 'col', axis=0)]
    all_to_all x1 -> x0, blocking collectives: 80.8 us -> none  [per_device(): lax.all_to_all(spread, 'row', split_axis=0, concat_axis=0, tiled=True)]
    all_to_all x1, waiting for transfers between devices: 7.83 us -> 28.7 us  [per_device(): lax.all_to_all(col_mean.reshape(count, rows_here, columns, heads * HS), '...]
    all_gather x1, waiting for transfers between devices: 13.1 us -> 0.02 us  [per_device(): piece_out = lax.all_gather(out_weight, 'row', axis=0, tiled=True)]
    all_gather x1, waiting for transfers between devices: 9.21 us -> 0.01 us  [per_device(): row_signal = lax.all_gather(signal, 'col', axis=0)]
  transfers between devices with their start and end apart: 6 -> 4, of which waited for: 6 -> 2; matrix products, arithmetic and copies ran while one was open for 1% -> 1% of each run, Pallas kernels for 19% -> 60%
where the time goes in v2:
time: 320 us
  Pallas kernels  203 us (63%)
  waiting for transfers between devices  85.7 us (27%)
  between operations  13.2 us (4%)
  blocking collectives  10.4 us (3%)
  starting transfers between devices  3.87 us (1%)
  local copies, waits for them, and re-layouts  3.48 us (1%)
    pallas_call x1, Pallas kernels, arrive(): pl.pallas_call(functools.partial(arrive_kernel, count=count, pieces=piece...  116 us
    all_gather x1, waiting for transfers between devices, per_device(): return project(lax.all_gather(attended, 'col', axis=0), piece_out, signal)  55.5 us
    pallas_call x2, Pallas kernels, norm_project(): pl.pallas_call(norm_project_kernel, out_shape=jax.ShapeDtypeStruct((token...  44.8 us
    all_to_all x1, waiting for transfers between devices, per_device(): lax.all_to_all(col_mean.reshape(count, rows_here, columns, heads * HS), '...  28.7 us
    pallas_call x1, Pallas kernels, row_attention(): pl.pallas_call(functools.partial(row_kernel, heads=heads, block=block_of(...  15 us
    pallas_call x1, Pallas kernels, project(): pl.pallas_call(project_kernel, out_shape=jax.ShapeDtypeStruct((tokens, ou...  10.7 us
    all_to_all x1, blocking collectives, per_device(): lax.all_to_all(col_stats, 'row', split_axis=0, concat_axis=2, tiled=True)  10.4 us
    pallas_call x1, Pallas kernels, column_attention(): pl.pallas_call(functools.partial(column_kernel, heads=heads), out_shape=(...  10.1 us
  transfers between devices with their start and end apart: 4, of which 2 were waited for; matrix products, arithmetic and copies ran while one was open for 1% of the time, Pallas kernels for 60%

profile of v2, /device:TPU:0, one launch (start us, length us, event | category | flops | bytes accessed | tf_op | source)
XLA Modules:
  0.0 319.8 jit_solution(15977184779408915536)
XLA Ops:
  6.5 0.0 all-gather.8.cloned.1.call-start
  6.5 0.7 all-gather.8.cloned.1.call-update
  7.3 116.4 %shard_map.46 = (bf16[4,16,128,512]{3,2,1,0:T(8,128)(2,1)}, bf16[2048,1536]{1,0:T(8,128)(2,1)}) custom-call(bf16[2,8,128,512]{3,2,1,0:T(8,128)(2,1)} %bitcast.18, bf16[256,1536]{1,0:T(8,128)(2,1)} %weight_ref.1), custom_call_target="tpu_custom_call" | custom-call | bytes 314572800 | tf_op jit(solution)/shard_map/pallas_call | solution.py:428
  123.6 22.4 %shard_map.49 = bf16[2048,1536]{1,0:T(8,128)(2,1)} custom-call(bf16[4,2048,512]{2,1,0:T(8,128)(2,1)} %bitcast.26, f32[1,2048]{1,0:T(1,128)} %bitcast.27, bf16[2048,1536]{1,0:T(8,128)(2,1)} %get-tuple-element.11.weight_ref), custom_call_target="tpu_custom_call" | custom-call | flops 12884901888 | bytes 20971520 | tf_op jit(solution)/shard_map/pallas_call | solution.py:51
  146.1 10.1 %shard_map.50 = (bf16[16,128,512]{2,1,0:T(8,128)(2,1)}, f32[8,8,256]{2,1,0:T(8,128)}) custom-call(bf16[16,128,1536]{2,1,0:T(8,128)(2,1)} %bitcast.20), custom_call_target="tpu_custom_call" | custom-call | tf_op jit(solution)/shard_map/pallas_call | solution.py:169
  156.2 1.0 reshape.27
  157.2 0.3 copy.9
  157.5 0.2 reshape.28
  157.7 10.4 %all_to_all.23 = f32[16,8,128]{2,1,0:T(8,128)S(1)} all-to-all(f32[16,8,128]{2,1,0:T(8,128)S(1)} %reshape.28), channel_id=1, replica_groups=mesh['row'=8,'col'=4] {'row'}, dimensions={0} | all-to-all | bytes 131072 | tf_op jit(solution)/shard_map/all_to_all | solution.py:468
  168.1 3.6 %all-to-all-start = ((bf16[8,2,128,512]{3,2,1,0:T(8,128)(2,1)}), bf16[8,2,128,512]{3,2,1,0:T(8,128)(2,1)S(1)}, u32[]{:S(2)}, u32[]{:S(2)}) async-start(bf16[8,2,128,512]{3,2,1,0:T(8,128)(2,1)} %bitcast.21), calls=%async_computation | async-start | bytes 4194304 | tf_op jit(solution)/shard_map/all_to_all | solution.py:469
  171.7 0.0 all-gather.6.cloned.1.call-start
  171.7 0.7 all-gather.6.cloned.1.call-update
  172.4 0.2 all-gather.10.cloned.1.call-start
  172.7 0.6 copy.10
  173.3 0.0 all-gather.8.cloned.1.call-done
  173.3 22.4 %shard_map.47.qkv_ref = bf16[2048,1536]{1,0:T(8,128)(2,1)} custom-call(bf16[4,2048,512]{2,1,0:T(8,128)(2,1)} %bitcast.25, f32[1,2048]{1,0:T(1,128)} %bitcast.28, bf16[2048,1536]{1,0:T(8,128)(2,1)} %get-tuple-element.11.weight_ref), custom_call_target="tpu_custom_call" | custom-call | flops 12884901888 | bytes 20971520 | tf_op jit(solution)/shard_map/pallas_call | solution.py:51
  195.7 15.0 %shard_map.48 = (f32[2048,512]{1,0:T(8,128)}, f32[2048,128]{1,0:T(8,128)}) custom-call(bf16[2048,1536]{1,0:T(8,128)(2,1)} %shard_map.47.qkv_ref), custom_call_target="tpu_custom_call" | custom-call | flops 4294967296 | bytes 10485760 | tf_op jit(solution)/shard_map/pallas_call | solution.py:116
  210.7 28.7 %all-to-all-done.mean_ref = bf16[8,2,128,512]{3,2,1,0:T(8,128)(2,1)S(1)} async-done(((bf16[8,2,128,512]{3,2,1,0:T(8,128)(2,1)}), bf16[8,2,128,512]{3,2,1,0:T(8,128)(2,1)S(1)}, u32[]{:S(2)}, u32[]{:S(2)}) %all-to-all-start) | async-done | bytes 2097184 | tf_op jit(solution)/shard_map/all_to_all | solution.py:469
  239.4 0.0 copy-start
  239.4 1.3 copy-done
  240.7 6.2 %shard_map.51 = bf16[2048,512]{1,0:T(8,128)(2,1)} custom-call(f32[2048,512]{1,0:T(8,128)} %get-tuple-element.12.acc_ref, f32[2048,128]{1,0:T(8,128)} %get-tuple-element.13.rstat_ref, bf16[8,2,128,512]{3,2,1,0:T(8,128)(2,1)} %copy-done, f32[2,8,1024]{2,1,0:T(8,128)} %bitcast.23), custom_call_target="tpu_custom_call" | custom-call | tf_op jit(solution)/shard_map/pallas_call | solution.py:213
  246.9 0.0 all-gather.10.cloned.1.call-update
  246.9 0.0 all-gather.6.cloned.1.call-done.weight_ref
  247.0 55.5 %all-gather.10.cloned.1.call-done = bf16[8192,512]{1,0:T(8,128)(2,1)} async-done(((bf16[2048,512]{1,0:T(8,128)(2,1)}), bf16[8192,512]{1,0:T(8,128)(2,1)}) %all-gather.10.cloned.1.call-update) | async-done | bytes 8388624 | tf_op jit(solution)/shard_map/all_gather | solution.py:479
  302.5 10.7 %shard_map.52 = bf16[2048,512]{1,0:T(8,128)(2,1)} custom-call(bf16[4,2048,512]{2,1,0:T(8,128)(2,1)} %bitcast.19, bf16[2048,512]{1,0:T(8,128)(2,1)} %all-gather.6.cloned.1.call-done.weight_ref, bf16[2048,512]{1,0:T(8,128)(2,1)} %signal_ref.1), custom_call_target="tpu_custom_call" | custom-call | tf_op jit(solution)/shard_map/pallas_call | solution.py:239
Async XLA Ops:
  6.5 166.8 %all-gather.8.cloned.1.call-start = ((), (), s32[]{:S(2)}) async-start(), calls=%async_computation.3 | async-start | bytes 10485760 | tf_op jit(solution)/shard_map/all_gather | solution.py:458
  168.1 71.3 %all-to-all-start = ((bf16[8,2,128,512]{3,2,1,0:T(8,128)(2,1)}), bf16[8,2,128,512]{3,2,1,0:T(8,128)(2,1)S(1)}, u32[]{:S(2)}, u32[]{:S(2)}) async-start(bf16[8,2,128,512]{3,2,1,0:T(8,128)(2,1)} %bitcast.21), calls=%async_computation | async-start | bytes 4194304 | tf_op jit(solution)/shard_map/all_to_all | solution.py:469
  171.7 75.3 %all-gather.6.cloned.1.call-start = ((), (), s32[]{:S(2)}) async-start(), calls=%async_computation.2 | async-start | bytes 2359296 | tf_op jit(solution)/shard_map/all_gather | solution.py:459
  172.4 130.1 %all-gather.10.cloned.1.call-start = ((), (), s32[]{:S(2)}) async-start(), calls=%async_computation.4 | async-start | bytes 10485760 | tf_op jit(solution)/shard_map/all_gather | solution.py:479
  239.4 1.3 copy-start
Sparse Core Ops, SparseCore 0:
  8.9 82.8 all-gather.7
  174.6 69.8 all-gather.5
  247.1 55.4 all-gather.9

commit v3 on v2

--- a/solution.py
+++ b/solution.py
@@ -204,50 +204,6 @@
         out_ref[:, across] = (
             (row_factor * share) * acc_ref[:, across] + (col_part * share) * mean
         ).astype(BF16)
-
-
-def merge(row_acc, row_stats, col_mean, col_stats, heads):
-    tokens, width = row_acc.shape
-    sources, _, columns, _ = col_mean.shape
-    held = col_stats.shape[1]
-    return pl.pallas_call(
-        functools.partial(merge_kernel, heads=heads),
-        out_shape=jax.ShapeDtypeStruct((tokens, width), BF16),
-        grid=(tokens // COLS,),
-        in_specs=[
-            pl.BlockSpec((COLS, width), lambda i: (i, 0)),
-            pl.BlockSpec((COLS, LANES), lambda i: (i, 0)),
-            pl.BlockSpec((sources, 1, columns, width), lambda i: (0, i, 0, 0)),
-            pl.BlockSpec((1, held, COLS), lambda i: (i, 0, 0)),
-        ],
-        out_specs=pl.BlockSpec((COLS, width), lambda i: (i, 0)),
-        compiler_params=pltpu.CompilerParams(vmem_limit_bytes=VMEM_LIMIT),
-    )(row_acc, row_stats, col_mean, col_stats)
-
-
-def project_kernel(att_ref, weight_ref, signal_ref, out_ref):
-    pieces, _, width = att_ref.shape
-    joined = jnp.concatenate([att_ref[i] for i in range(pieces)], axis=1)
-    branch = jnp.dot(joined, weight_ref[...], preferred_element_type=F32)
-    out_ref[...] = (signal_ref[...].astype(F32) + branch).astype(BF16)
-
-
-def project(gathered, weight, signal):
-    pieces, tokens, width = gathered.shape
-    features, outs = weight.shape
-    block = block_of(tokens, 256)
-    return pl.pallas_call(
-        project_kernel,
-        out_shape=jax.ShapeDtypeStruct((tokens, outs), BF16),
-        grid=(tokens // block,),
-        in_specs=[
-            pl.BlockSpec((pieces, block, width), lambda i: (0, i, 0)),
-            pl.BlockSpec((features, outs), lambda i: (0, 0)),
-            pl.BlockSpec((block, outs), lambda i: (i, 0)),
-        ],
-        out_specs=pl.BlockSpec((block, outs), lambda i: (i, 0)),
-        compiler_params=pltpu.CompilerParams(vmem_limit_bytes=VMEM_LIMIT),
-    )(gathered, weight, signal)
 
 
 def remote(src, dst, sems, at, target):
@@ -441,6 +397,112 @@
     )(signal, weight)
 
 
+def finish_kernel(
+    acc_ref,
+    rstat_ref,
+    mean_ref,
+    cstat_ref,
+    weight_ref,
+    signal_ref,
+    out_ref,
+    held_ref,
+    peer_send,
+    peer_recv,
+    twin_send,
+    twin_recv,
+    *,
+    heads,
+    block,
+):
+    row, col = lax.axis_index("row"), lax.axis_index("col")
+    pieces, tokens, _ = held_ref.shape
+    chips = pieces // 2
+    twin = (row, col + 1 - 2 * (col % 2))
+    peers = [(row, (col + 2 * k) % pieces) for k in range(1, chips)]
+    barrier = pltpu.get_barrier_semaphore()
+    for target in peers + [twin]:
+        pl.semaphore_signal(
+            barrier, inc=1, device_id=target, device_id_type=pl.DeviceIdType.MESH
+        )
+    pl.semaphore_wait(barrier, len(peers) + 1)
+
+    started = []
+
+    def send(at, owner, sems, index, target):
+        piece = held_ref.at[owner, pl.ds(at * block, block)]
+        copy = remote(piece, piece, sems, index, target)
+        copy.start()
+        started.append(copy)
+        return copy
+
+    arriving, passed = [], []
+    for line in range(tokens // COLS):
+        rows = pl.ds(line * COLS, COLS)
+        merge_kernel(
+            acc_ref.at[rows],
+            rstat_ref.at[rows],
+            mean_ref.at[:, pl.ds(line, 1)],
+            cstat_ref.at[pl.ds(line, 1)],
+            held_ref.at[col, rows],
+            heads=heads,
+        )
+        for at in range(line * COLS // block, (line + 1) * COLS // block):
+            arriving.append(
+                [
+                    send(at, col, (peer_send, peer_recv), at * (chips - 1) + j, target)
+                    for j, target in enumerate(peers)
+                ]
+            )
+            passed.append([send(at, col, (twin_send, twin_recv), at * chips, twin)])
+
+    def multiply(at):
+        for copy in passed[at]:
+            copy.wait_recv()
+        rows = pl.ds(at * block, block)
+        joined = jnp.concatenate([held_ref[i, rows, :] for i in range(pieces)], axis=1)
+        branch = jnp.dot(joined, weight_ref[...], preferred_element_type=F32)
+        out_ref[rows, :] = (signal_ref[rows, :].astype(F32) + branch).astype(BF16)
+
+    for at in range(tokens // block):
+        for j, copy in enumerate(arriving[at]):
+            copy.wait_recv()
+            owner = (col + pieces - 2 * (j + 1)) % pieces
+            passed[at].append(
+                send(at, owner, (twin_send, twin_recv), at * chips + 1 + j, twin)
+            )
+        if at > 0:
+            multiply(at - 1)
+    multiply(tokens // block - 1)
+    for copy in started:
+        copy.wait_send()
+
+
+def finish(row_acc, row_stats, col_mean, col_stats, weight, signal, heads, pieces):
+    tokens, width = row_acc.shape
+    outs = weight.shape[1]
+    block = block_of(COLS, 256)
+    chips = pieces // 2
+    chunks = tokens // block
+    dma = pltpu.SemaphoreType.DMA
+    sizes = (max(1, chunks * (chips - 1)), chunks * chips)
+    return pl.pallas_call(
+        functools.partial(finish_kernel, heads=heads, block=block),
+        out_shape=jax.ShapeDtypeStruct((tokens, outs), BF16),
+        in_specs=[pl.BlockSpec(memory_space=pltpu.VMEM)] * 6,
+        out_specs=pl.BlockSpec(memory_space=pltpu.VMEM),
+        scratch_shapes=[pltpu.VMEM((pieces, tokens, width), BF16)]
+        + [dma((size,)) for size in sizes for _ in range(2)],
+        compiler_params=pltpu.CompilerParams(
+            collective_id=1, has_side_effects=True, vmem_limit_bytes=VMEM_LIMIT
+        ),
+        cost_estimate=pl.CostEstimate(
+            flops=2 * tokens * pieces * width * outs,
+            bytes_accessed=150 * 1024 * 1024,
+            transcendentals=0,
+        ),
+    )(row_acc, row_stats, col_mean, col_stats, weight, signal)
+
+
 def per_device(signal, norm_gain, qkv_weight, out_weight):
     samples, width = signal.shape
     count = lax.axis_size("row")
@@ -475,8 +537,9 @@
     )
     row_qkv = norm_project(row_signal, norm_gain, piece_qkv)
     row_acc, row_stats = row_attention(row_qkv, heads)
-    attended = merge(row_acc, row_stats, col_mean, col_stats, heads)
-    return project(lax.all_gather(attended, "col", axis=0), piece_out, signal)
+    return finish(
+        row_acc, row_stats, col_mean, col_stats, piece_out, signal, heads, pieces
+    )
 
 
 def solution(mesh):

time: 320 us -> 312 us (0.975)
  waiting for transfers between devices: 85.7 us -> 35.5 us
  Pallas kernels: 203 us -> 243 us
    all_gather x1 -> x0, waiting for transfers between devices: 55.5 us -> none  [per_device(): return project(lax.all_gather(attended, 'col', axis=0), piece_out, signal)]
    pallas_call x2 -> x1, Pallas kernels: 16.9 us -> 56.8 us  [finish(): pl.pallas_call(functools.partial(finish_kernel, heads=heads, block=block)...]
    all_gather x1, waiting for transfers between devices: 0.02 us -> 5.14 us  [per_device(): piece_out = lax.all_gather(out_weight, 'row', axis=0, tiled=True)]
  transfers between devices with their start and end apart: 4 -> 3, of which waited for: 2 -> 2; matrix products, arithmetic and copies ran while one was open for 1% -> 1% of each run, Pallas kernels for 60% -> 60%
where the time goes in v3:
time: 312 us; the launch traced here: 311 us
  Pallas kernels  243 us (78%)
  waiting for transfers between devices  35.5 us (11%)
  between operations  13.4 us (4%)
  blocking collectives  10.3 us (3%)
  local copies, waits for them, and re-layouts  5.2 us (2%)
  starting transfers between devices  3.65 us (1%)
    pallas_call x1, Pallas kernels, arrive(): pl.pallas_call(functools.partial(arrive_kernel, count=count, pieces=piece...  116 us
    pallas_call x1, Pallas kernels, finish(): pl.pallas_call(functools.partial(finish_kernel, heads=heads, block=block)...  56.8 us
    pallas_call x2, Pallas kernels, norm_project(): pl.pallas_call(norm_project_kernel, out_shape=jax.ShapeDtypeStruct((token...  44.8 us
    all_to_all x1, waiting for transfers between devices, per_device(): lax.all_to_all(col_mean.reshape(count, rows_here, columns, heads * HS), '...  29 us
    pallas_call x1, Pallas kernels, row_attention(): pl.pallas_call(functools.partial(row_kernel, heads=heads, block=block_of(...  15 us
    all_to_all x1, blocking collectives, per_device(): lax.all_to_all(col_stats, 'row', split_axis=0, concat_axis=2, tiled=True)  10.3 us
    pallas_call x1, Pallas kernels, column_attention(): pl.pallas_call(functools.partial(column_kernel, heads=heads), out_shape=(...  10.1 us
  transfers between devices with their start and end apart: 3, of which 2 were waited for; matrix products, arithmetic and copies ran while one was open for 1% of the time, Pallas kernels for 60%

profile of v3, /device:TPU:0, one launch (start us, length us, event | category | flops | bytes accessed | tf_op | source)
XLA Modules:
  0.0 311.2 jit_solution(15878576865523780463)
XLA Ops:
  6.5 0.0 all-gather.6.cloned.1.call-start
  6.5 0.7 all-gather.6.cloned.1.call-update
  7.3 116.4 %shard_map.46 = (bf16[4,16,128,512]{3,2,1,0:T(8,128)(2,1)}, bf16[2048,1536]{1,0:T(8,128)(2,1)}) custom-call(bf16[2,8,128,512]{3,2,1,0:T(8,128)(2,1)} %bitcast.17, bf16[256,1536]{1,0:T(8,128)(2,1)} %weight_ref.1), custom_call_target="tpu_custom_call" | custom-call | bytes 314572800 | tf_op jit(solution)/shard_map/pallas_call | solution.py:384
  123.6 22.4 %shard_map.49 = bf16[2048,1536]{1,0:T(8,128)(2,1)} custom-call(bf16[4,2048,512]{2,1,0:T(8,128)(2,1)} %bitcast.24, f32[1,2048]{1,0:T(1,128)} %bitcast.25, bf16[2048,1536]{1,0:T(8,128)(2,1)} %get-tuple-element.11.weight_ref), custom_call_target="tpu_custom_call" | custom-call | flops 12884901888 | bytes 20971520 | tf_op jit(solution)/shard_map/pallas_call | solution.py:51
  146.1 10.1 %shard_map.50 = (bf16[16,128,512]{2,1,0:T(8,128)(2,1)}, f32[8,8,256]{2,1,0:T(8,128)}) custom-call(bf16[16,128,1536]{2,1,0:T(8,128)(2,1)} %bitcast.18), custom_call_target="tpu_custom_call" | custom-call | tf_op jit(solution)/shard_map/pallas_call | solution.py:169
  156.2 1.0 reshape.27
  157.2 0.3 copy.9
  157.5 0.2 reshape.28
  157.7 10.3 %all_to_all.23 = f32[16,8,128]{2,1,0:T(8,128)S(1)} all-to-all(f32[16,8,128]{2,1,0:T(8,128)S(1)} %reshape.28), channel_id=1, replica_groups=mesh['row'=8,'col'=4] {'row'}, dimensions={0} | all-to-all | bytes 131072 | tf_op jit(solution)/shard_map/all_to_all | solution.py:530
  168.1 3.6 %all-to-all-start = ((bf16[8,2,128,512]{3,2,1,0:T(8,128)(2,1)}), bf16[8,2,128,512]{3,2,1,0:T(8,128)(2,1)S(1)}, u32[]{:S(2)}, u32[]{:S(2)}) async-start(bf16[8,2,128,512]{3,2,1,0:T(8,128)(2,1)} %bitcast.19), calls=%async_computation | async-start | bytes 4194304 | tf_op jit(solution)/shard_map/all_to_all | solution.py:531
  171.7 0.0 all-gather.4.cloned.1.call-start
  171.7 0.7 all-gather.4.cloned.1.call-update
  172.4 0.6 copy.10
  173.1 0.0 all-gather.6.cloned.1.call-done
  173.1 22.4 %shard_map.47.qkv_ref = bf16[2048,1536]{1,0:T(8,128)(2,1)} custom-call(bf16[4,2048,512]{2,1,0:T(8,128)(2,1)} %bitcast.23, f32[1,2048]{1,0:T(1,128)} %bitcast.26, bf16[2048,1536]{1,0:T(8,128)(2,1)} %get-tuple-element.11.weight_ref), custom_call_target="tpu_custom_call" | custom-call | flops 12884901888 | bytes 20971520 | tf_op jit(solution)/shard_map/pallas_call | solution.py:51
  195.4 15.0 %shard_map.48 = (f32[2048,512]{1,0:T(8,128)}, f32[2048,128]{1,0:T(8,128)}) custom-call(bf16[2048,1536]{1,0:T(8,128)(2,1)} %shard_map.47.qkv_ref), custom_call_target="tpu_custom_call" | custom-call | flops 4294967296 | bytes 10485760 | tf_op jit(solution)/shard_map/pallas_call | solution.py:116
  210.4 29.0 %all-to-all-done.mean_ref = bf16[8,2,128,512]{3,2,1,0:T(8,128)(2,1)S(1)} async-done(((bf16[8,2,128,512]{3,2,1,0:T(8,128)(2,1)}), bf16[8,2,128,512]{3,2,1,0:T(8,128)(2,1)S(1)}, u32[]{:S(2)}, u32[]{:S(2)}) %all-to-all-start) | async-done | bytes 2097184 | tf_op jit(solution)/shard_map/all_to_all | solution.py:531
  239.4 0.0 copy-start
  239.4 5.1 %all-gather.4.cloned.1.call-done.weight_ref = bf16[2048,512]{1,0:T(8,128)(2,1)} async-done(((bf16[256,512]{1,0:T(8,128)(2,1)}), bf16[2048,512]{1,0:T(8,128)(2,1)}) %all-gather.4.cloned.1.call-update) | async-done | bytes 2097168 | tf_op jit(solution)/shard_map/all_gather | solution.py:521
  244.5 0.0 copy-done
  244.6 56.8 %shard_map.51 = bf16[2048,512]{1,0:T(8,128)(2,1)} custom-call(f32[2048,512]{1,0:T(8,128)} %get-tuple-element.12.acc_ref, f32[2048,128]{1,0:T(8,128)} %get-tuple-element.13.rstat_ref, bf16[8,2,128,512]{3,2,1,0:T(8,128)(2,1)} %copy-done, f32[2,8,1024]{2,1,0:T(8,128)} %bitcast.22, bf16[2048,512]{1,0:T(8,128)(2,1)} %all-gather.4.cloned.1.call-done.weight_ref, ...), custom_call_target="tpu_custom_call" | custom-call | flops 4294967296 | bytes 157286400 | tf_op jit(solution)/shard_map/pallas_call | solution.py:488
  301.3 3.0 copy.12
Async XLA Ops:
  6.5 166.5 %all-gather.6.cloned.1.call-start = ((), (), s32[]{:S(2)}) async-start(), calls=%async_computation.3 | async-start | bytes 10485760 | tf_op jit(solution)/shard_map/all_gather | solution.py:520
  168.1 71.3 %all-to-all-start = ((bf16[8,2,128,512]{3,2,1,0:T(8,128)(2,1)}), bf16[8,2,128,512]{3,2,1,0:T(8,128)(2,1)S(1)}, u32[]{:S(2)}, u32[]{:S(2)}) async-start(bf16[8,2,128,512]{3,2,1,0:T(8,128)(2,1)} %bitcast.19), calls=%async_computation | async-start | bytes 4194304 | tf_op jit(solution)/shard_map/all_to_all | solution.py:531
  171.7 72.9 %all-gather.4.cloned.1.call-start = ((), (), s32[]{:S(2)}) async-start(), calls=%async_computation.2 | async-start | bytes 2359296 | tf_op jit(solution)/shard_map/all_gather | solution.py:521
  239.4 5.1 %copy-start = (bf16[8,2,128,512]{3,2,1,0:T(8,128)(2,1)}, bf16[8,2,128,512]{3,2,1,0:T(8,128)(2,1)S(1)}, u32[]{:S(2)}) copy-start(bf16[8,2,128,512]{3,2,1,0:T(8,128)(2,1)S(1)} %all-to-all-done.mean_ref) | copy-start | bytes 6291460
Sparse Core Ops, SparseCore 0:
  8.9 82.8 all-gather.5
  174.6 69.8 all-gather.3
